TPU v7x, 256 devices: a whole 4x4x8 slice. The times are simulated.
256 devices in a mesh: grp: 8 (over z_hi, core), tile: 32 (over x, y, z_lo).
Axes of the slice: x: 4, y: 4, z: 8 (z_hi: 4, z_lo: 2; z = z_hi * 2 + z_lo), core: 2. Of those that a mesh axis runs over, the one named last changes fastest.
Arguments:
- right_side: float32 [256, 16384], P('grp', 'tile'), may hold values from -8 to 8
- diagonal: float32 [256, 16384], P('grp', 'tile'), may hold values from 0.25 to 2
- inverse_factor: float32 [16384, 16384], P(('grp', 'tile')), may hold values from -2 to 2, as said below
Outputs:
- solution_field: float32 [256, 16384], P('grp', 'tile')
Inputs may be any that keep to these rules, and one draw needn't show every extreme that they name: `inverse_factor`: zero above the diagonal; the diagonal lies between 1 and 2.
All inputs are finite; a program needn't handle non-finite values.
Results may differ from a plain program's by a relative error of at most 0.0003.
Values sent between devices are 32-bit elements; how exact they have to be, the bound alone decides.
A program may use at most 64 MiB of HBM per device.

v0:
```python
import jax
import jax.numpy as jnp
from jax import lax
from jax.sharding import PartitionSpec as P

FAC = 16
SWEEPS = 4
CYCLES = 2


def extended(block, sides, width):
    for axis, dim in sides:
        count = lax.axis_size(axis)
        forward = [(i, i + 1) for i in range(count - 1)]
        backward = [(target, source) for source, target in forward]
        low = lax.ppermute(
            lax.slice_in_dim(block, block.shape[dim] - width, None, axis=dim), axis, forward
        )
        high = lax.ppermute(lax.slice_in_dim(block, 0, width, axis=dim), axis, backward)
        block = jnp.concatenate([low, block, high], axis=dim)
    return block


def operate(field, diagonal):
    padded = extended(field, (("grp", 0), ("tile", 1)), 1)
    beside = padded[2:, 1:-1] + padded[:-2, 1:-1] + padded[1:-1, 2:] + padded[1:-1, :-2]
    beside = beside + padded[2:, :-2] + padded[:-2, 2:]
    return (6.0 + diagonal) * field - beside


def shards(right_side, diagonal, inverse_factor):
    rows_here, cols_here = right_side.shape
    coarse_here = inverse_factor.shape[0]
    scale = 1.0 / (6.0 + diagonal)
    solution_field = jnp.zeros_like(right_side)
    for cycle in range(CYCLES):
        if cycle == 0:
            residual = right_side
        else:
            residual = right_side - operate(solution_field, diagonal)
        smoothed = None
        coarse_rhs = jnp.mean(
            residual.reshape(rows_here // FAC, FAC, cols_here // FAC, FAC), axis=(1, 3)
        ).reshape(-1)
        inner = jnp.dot(
            inverse_factor,
            lax.all_gather(coarse_rhs, ("grp", "tile"), axis=0, tiled=True),
            precision=lax.Precision.HIGHEST,
        )
        smoothed = 0.8 * residual * scale
        for sweep in range(SWEEPS - 1):
            smoothed = smoothed + 0.8 * (residual - operate(smoothed, diagonal)) * scale
        whole_term = jnp.dot(inner, inverse_factor, precision=lax.Precision.HIGHEST)
        summed = lax.psum(whole_term, ("grp", "tile"))
        offset = lax.axis_index(("grp", "tile")) * coarse_here
        coarse_fix = lax.dynamic_slice_in_dim(summed, offset, coarse_here, 0)
        blocks = coarse_fix.reshape(rows_here // FAC, 1, cols_here // FAC, 1)
        spread_fix = jnp.broadcast_to(
            blocks, (rows_here // FAC, FAC, cols_here // FAC, FAC)
        ).reshape(rows_here, cols_here)
        solution_field = solution_field + smoothed + 0.5 * spread_fix
    return solution_field


def solution(mesh):
    placed = (P("grp", "tile"), P("grp", "tile"), P(("grp", "tile"), None))
    return jax.shard_map(
        shards, mesh=mesh, in_specs=placed, out_specs=P("grp", "tile"), check_vma=False
    )
```

profile of v0, /device:TPU:1, one launch (start us, length us, event | category | flops | bytes accessed | tf_op | source)
XLA Modules:
  0.0 1096.1 jit_solution(2937678232551976307)
XLA Ops:
  6.5 0.9 multiply_multiply_fusion.1
  7.4 5.1 collective-permute-start
  12.6 3.1 collective-permute-start.1
  15.7 0.7 collective-permute-done.1
  16.5 3.5 collective-permute-start.3
  20.0 1.3 collective-permute-start.2
  21.3 3.2 collective-permute-done.2
  24.6 1.0 fusion.40
  25.6 1.9 collective-permute-start.4
  27.6 6.5 collective-permute-start.5
  34.1 1.0 reshape.28
  35.2 3.7 collective-permute-start.7
  38.9 1.3 collective-permute-start.6
  40.2 0.1 reduce_sum.18
  40.4 3.1 collective-permute-done.6
  43.6 1.0 fusion.34
  44.6 1.9 collective-permute-start.8
  46.5 6.2 collective-permute-start.9
  52.8 0.2 dynamic-update-slice
  53.0 0.6 copy-done.5
  53.8 3.5 collective-permute-start.11
  57.3 1.3 collective-permute-start.10
  58.6 239.1 %all-reduce.11.cloned.1.call-done = f32[16384]{0:T(1024)} async-done(((f32[16384]{0:T(1024)}), f32[16384]{0:T(1024)}) %all-reduce.11.cloned.1.call-update) | async-done | bytes 65552
  297.8 5.7 convolution_bitcast_fusion.1
  303.5 2.7 fusion.50
  306.4 234.0 %all-reduce.7.cloned.1.call-done = f32[16384]{0:T(1024)} async-done(((f32[16384]{0:T(1024)}), f32[16384]{0:T(1024)}) %all-reduce.7.cloned.1.call-update) | async-done | bytes 65552 | tf_op jit(solution)/shard_map/psum | solution.py:54
  540.4 0.8 dynamic-slice_multiply_fusion.1
  541.2 0.1 broadcast_in_dim.4
  541.4 0.3 mul.112
  541.7 0.1 fusion.28
  541.8 1.9 collective-permute-start.12
  543.7 4.5 collective-permute-start.13
  548.3 0.7 collective-permute-done.13
  549.1 3.7 collective-permute-start.15
  552.7 1.3 collective-permute-start.14
  554.0 3.2 collective-permute-done.14
  557.5 1.9 collective-permute-start.16
  559.4 6.5 collective-permute-start.17
  566.0 0.7 collective-permute-done.17
  566.7 2.8 collective-permute-start.19
  569.5 1.3 collective-permute-start.18
  570.8 3.2 collective-permute-done.18
  574.3 1.9 collective-permute-start.20
  576.2 6.5 collective-permute-start.21
  582.7 0.2 reshape.29
  582.9 0.5 collective-permute-done.21
  583.5 3.5 collective-permute-start.23
  587.0 1.3 collective-permute-start.22
  588.3 0.1 reduce_sum.19
  588.5 3.1 collective-permute-done.22
  591.8 1.9 collective-permute-start.24
  593.7 6.6 collective-permute-start.25
  600.5 0.2 dynamic-update-slice.1
  600.7 0.6 copy-done.4
  601.5 3.1 collective-permute-start.27
  604.6 1.5 collective-permute-start.26
  606.1 238.9 %all-reduce.13.cloned.1.call-done = f32[16384]{0:T(1024)} async-done(((f32[16384]{0:T(1024)}), f32[16384]{0:T(1024)}) %all-reduce.13.cloned.1.call-update) | async-done | bytes 65552
  844.9 5.7 convolution_bitcast_fusion
  850.6 2.7 fusion.51
  853.5 234.1 %all-reduce.9.cloned.1.call-done = f32[16384]{0:T(1024)} async-done(((f32[16384]{0:T(1024)}), f32[16384]{0:T(1024)}) %all-reduce.9.cloned.1.call-update) | async-done | bytes 65552 | tf_op jit(solution)/shard_map/psum | solution.py:54
  1087.6 0.8 dynamic-slice_multiply_fusion
  1088.4 0.1 broadcast_in_dim.5
  1088.6 0.3 mul.127
  1088.8 0.7 fusion.6
  (69 shorter events, 2.2 us)
Async XLA Ops:
  6.5 291.2 %all-reduce.11.cloned.1.call-start = ((), (), s32[]{:S(2)}) async-start(), calls=%async_computation.2 | async-start | bytes 131072
  7.4 8.2 collective-permute-start
  12.6 3.8 collective-permute-start.1
  16.5 4.8 collective-permute-start.3
  20.0 4.5 collective-permute-start.2
  25.6 9.5 collective-permute-start.4
  27.6 7.6 collective-permute-start.5
  35.2 5.1 collective-permute-start.7
  38.9 4.5 collective-permute-start.6
  44.6 9.1 collective-permute-start.8
  46.5 7.2 collective-permute-start.9
  53.0 0.6 copy-start.5
  53.7 486.7 %all-reduce.7.cloned.1.call-start = ((), (), s32[]{:S(2)}) async-start(), calls=%async_computation | async-start | bytes 131072 | tf_op jit(solution)/shard_map/psum | solution.py:54
  53.8 252.4 %collective-permute-start.11 = (f32[34,1]{1,0:T(8,128)S(1)}, f32[34,1]{1,0:T(8,128)S(1)}, u32[]{:S(2)}, u32[]{:S(2)}) collective-permute-start(f32[34,1]{1,0:T(8,128)S(1)} %get-tuple-element.25), channel_id=1, source_target_pairs={{0,1},{1,2},{2,3},{3,4},{4,5},{5,6},{6,7},{7,8},{8,9},{9,10},{10,1... | collective-permute-start | bytes 416 | tf_op jit(solution)/shard_map/ppermute | solution.py:16
  57.3 249.0 %collective-permute-start.10 = (f32[34,1]{1,0:T(8,128)S(1)}, f32[34,1]{1,0:T(8,128)S(1)}, u32[]{:S(2)}, u32[]{:S(2)}) collective-permute-start(f32[34,1]{1,0:T(8,128)S(1)} %get-tuple-element.26), channel_id=1, source_target_pairs={{1,0},{2,1},{3,2},{4,3},{5,4},{6,5},{7,6},{8,7},{9,8},{10,9},{11,1... | collective-permute-start | bytes 416 | tf_op jit(solution)/shard_map/ppermute | solution.py:19
  297.7 5.7 copy-start
  297.7 243.9 %copy-start.2 = (f32[32,512]{1,0:T(8,128)S(1)}, f32[32,512]{1,0:T(8,128)}, u32[]{:S(2)}) copy-start(f32[32,512]{1,0:T(8,128)} %param.4) | copy-start | bytes 196612
  297.7 243.9 %copy-start.3 = (f32[32,512]{1,0:T(8,128)S(1)}, f32[32,512]{1,0:T(8,128)}, u32[]{:S(2)}) copy-start(f32[32,512]{1,0:T(8,128)} %param.3) | copy-start | bytes 196612
  306.2 538.7 %all-reduce.13.cloned.1.call-start = ((), (), s32[]{:S(2)}) async-start(), calls=%async_computation.3 | async-start | bytes 131072
  541.8 6.5 collective-permute-start.12
  543.7 5.3 collective-permute-start.13
  549.1 5.0 collective-permute-start.15
  552.7 4.5 collective-permute-start.14
  557.5 8.5 collective-permute-start.16
  559.4 7.2 collective-permute-start.17
  566.7 4.1 collective-permute-start.19
  569.5 4.5 collective-permute-start.18
  574.3 8.7 collective-permute-start.20
  576.2 7.2 collective-permute-start.21
  583.5 5.0 collective-permute-start.23
  587.0 4.5 collective-permute-start.22
  591.8 9.6 collective-permute-start.24
  593.7 7.7 collective-permute-start.25
  600.7 0.6 copy-start.4
  601.4 486.2 %all-reduce.9.cloned.1.call-start = ((), (), s32[]{:S(2)}) async-start(), calls=%async_computation.1 | async-start | bytes 131072 | tf_op jit(solution)/shard_map/psum | solution.py:54
  601.5 251.9 %collective-permute-start.27 = (f32[34,1]{1,0:T(8,128)S(1)}, f32[34,1]{1,0:T(8,128)S(1)}, u32[]{:S(2)}, u32[]{:S(2)}) collective-permute-start(f32[34,1]{1,0:T(8,128)S(1)} %get-tuple-element.9), channel_id=1, source_target_pairs={{0,1},{1,2},{2,3},{3,4},{4,5},{5,6},{6,7},{7,8},{8,9},{9,10},{10,1... | collective-permute-start | bytes 416 | tf_op jit(solution)/shard_map/ppermute | solution.py:16
  604.6 248.8 %collective-permute-start.26 = (f32[34,1]{1,0:T(8,128)S(1)}, f32[34,1]{1,0:T(8,128)S(1)}, u32[]{:S(2)}, u32[]{:S(2)}) collective-permute-start(f32[34,1]{1,0:T(8,128)S(1)} %get-tuple-element.10), channel_id=1, source_target_pairs={{1,0},{2,1},{3,2},{4,3},{5,4},{6,5},{7,6},{8,7},{9,8},{10,9},{11,1... | collective-permute-start | bytes 416 | tf_op jit(solution)/shard_map/ppermute | solution.py:19
  844.9 5.7 copy-start.1
Sparse Core Ops, SparseCore 0:
  53.8 243.9 all-reduce.10
  306.3 234.0 all-reduce.6
  601.5 243.4 all-reduce.12
  853.5 234.0 all-reduce.8
where the time goes:
time: 1100 us
  waiting for transfers between devices  965 us (88%)
  starting transfers between devices  89.7 us (8%)
  matrix products  16.9 us (2%)
  between operations  13.7 us (1%)
    unnamed x6, waiting for transfers between devices  478 us
    psum x2, waiting for transfers between devices, shards(): summed = lax.psum(whole_term, ('grp', 'tile'))  468 us
    ppermute x14, starting transfers between devices, extended(): lax.ppermute(lax.slice_in_dim(block, block.shape[dim] - width, None, axis...  63.7 us
    ppermute x14, starting transfers between devices, extended(): lax.ppermute(lax.slice_in_dim(block, 0, width, axis=dim), axis, backward)  25.9 us
  transfers between devices with their start and end apart: 32, of which 13 were waited for; matrix products, arithmetic and copies ran while one was open for 2% of the time, Pallas kernels for 0%

commit v1 on v0

v1 whole, which is shorter than its diff:
```python
import functools

import jax
import jax.numpy as jnp
from jax import lax
from jax.experimental import pallas as pl
from jax.experimental.pallas import tpu as pltpu
from jax.sharding import PartitionSpec as P

MESH = pl.DeviceIdType.MESH
HIGHEST = lax.Precision.HIGHEST
RD, CD, FAC = 32, 512, 16
N_GRP, N_TILE = 8, 32
HR, HC = 8, 128
ER, EC = RD + 2 * HR, CD + 2 * HC
CO = 64
N_LANE, N_Z = 32, 8
DIRECTIONS = [(a, b) for a in (-1, 0, 1) for b in (-1, 0, 1) if (a, b) != (0, 0)]


def device_at(m, z):
    return ((z // 2) * 2 + m // 16, (m % 16) * 2 + z % 2)


def beside(field):
    right = pltpu.roll(field, EC - 1, 1)
    left = pltpu.roll(field, 1, 1)
    return right + left + pltpu.roll(field + right, 1, 0) + pltpu.roll(field + left, ER - 1, 0)


def lanes(shape):
    return lax.broadcasted_iota(jnp.int32, shape, len(shape) - 1)


def restricted(block, z_lo):
    top = jnp.sum(block[:FAC], axis=0, keepdims=True)
    low = jnp.sum(block[FAC:], axis=0, keepdims=True)
    sums = jnp.concatenate([top, low, jnp.zeros((6, CD), jnp.float32)], axis=0)
    cell = lax.broadcasted_iota(jnp.int32, (CD, 128), 0) // FAC
    gather = jnp.where(cell == lanes((CD, 128)) % 32, 1.0 / (FAC * FAC), 0.0).astype(jnp.float32)
    means = jnp.dot(sums, gather, precision=HIGHEST, preferred_element_type=jnp.float32)
    lane = lanes((1, 128))
    row = jnp.where((lane // 32) % 2 == 0, means[0:1], means[1:2])
    return jnp.where(lane // 64 == z_lo, row, 0.0)


def spread_columns(rows):
    cell = lax.broadcasted_iota(jnp.int32, (128, CD), 0) % 32
    spread = jnp.where(cell == lanes((128, CD)) // FAC, 1.0, 0.0).astype(jnp.float32)
    return jnp.dot(rows, spread, precision=HIGHEST, preferred_element_type=jnp.float32)


def quarter(row, z_lo, i_hi, valid):
    lane = lanes((1, 128))
    keep = (lane // 32 == z_lo * 2 + i_hi) & valid
    return jnp.where(keep, row, 0.0)


def coarse_neighbours(field):
    sub = lax.broadcasted_iota(jnp.int32, (8, 128), 0)
    lane = lanes((8, 128))
    second = (lane // 32) % 2 == 1
    edge_hi, edge_lo = lane % 32 == 31, lane % 32 == 0
    z_hi_half = lane // 64 == 1
    straight, to_right, to_left = [], [], []
    for c in field:
        fwd = pltpu.roll(c, 32, 1)
        back = pltpu.roll(c, 96, 1)
        above = jnp.where(sub >= 4, pltpu.roll(back, 4, 0), pltpu.roll(back, 5, 0))
        above = jnp.where(sub == 0, 0.0, above)
        below = jnp.where(sub < 4, pltpu.roll(fwd, 4, 0), pltpu.roll(fwd, 3, 0))
        below = jnp.where(sub == 7, 0.0, below)
        up = jnp.where(second, fwd, above)
        down = jnp.where(second, below, back)
        straight.append(31.0 * (up + down))
        to_right.append(31.0 * c + up)
        to_left.append(31.0 * c + down)
    zero = jnp.zeros((8, 128), jnp.float32)
    far_right = [pltpu.roll(v, 95, 1) for v in to_right] + [zero]
    far_left = [zero] + [pltpu.roll(v, 33, 1) for v in to_left]
    total = []
    for i in range(16):
        right = jnp.where(z_hi_half, far_right[i + 1], far_right[i])
        right = jnp.where(edge_hi, right, pltpu.roll(to_right[i], 127, 1))
        left = jnp.where(z_hi_half, far_left[i + 1], far_left[i])
        left = jnp.where(edge_lo, left, pltpu.roll(to_left[i], 1, 1))
        total.append(straight[i] + right + left)
    return total


def column(tile):
    return pl.ds(pl.multiple_of(tile * 128, 128), 128)


def times_factor(factor, row_of):
    def step(xy, totals):
        totals = list(totals)
        for s in range(8):
            row = row_of(xy, s)
            where = column((s % 4) * 32 + (s // 4) * 16 + xy)
            for i in range(8):
                totals[i] = totals[i] + factor[pl.ds(8 * i, 8), where] * row
        return tuple(totals)

    zero = jnp.zeros((8, 128), jnp.float32)
    totals = lax.fori_loop(0, 16, step, (zero,) * 8)
    return [jnp.sum(v, axis=1, keepdims=True) for v in totals]


def kernel(
    right_ref, diag_ref, factor_ref, out_ref,
    cells, factor, smooth, scale_ref, result,
    row_ref, row_in, chunk_ref, chunk_in, term, term_in, part, part_in,
    fix, fix_in, rhs_ref, term_b, term_b_in, last, last_in,
    load_sem, halo_send, halo_recv, send_sem, recv_sem,
):
    g, t = lax.axis_index("grp"), lax.axis_index("tile")
    z_hi, core, xy, z_lo = g // 2, g % 2, t // 2, t % 2
    m, z = core * 16 + xy, z_hi * 2 + z_lo
    rows_in, cols_in = pl.ds(HR, RD), pl.ds(HC, CD)

    loads = [
        pltpu.make_async_copy(right_ref, cells.at[0, rows_in, cols_in], load_sem.at[0]),
        pltpu.make_async_copy(diag_ref, cells.at[1, rows_in, cols_in], load_sem.at[1]),
        pltpu.make_async_copy(factor_ref, factor, load_sem.at[2]),
    ]
    for load in loads:
        load.start()

    barrier = pltpu.get_barrier_semaphore()

    def greet_z(k, _):
        pl.semaphore_signal(
            barrier, 1, device_id=device_at(m, (z + 1 + k) % N_Z), device_id_type=MESH
        )
        return _

    def greet_m(k, _):
        pl.semaphore_signal(
            barrier, 1, device_id=device_at((m + 1 + k) % N_LANE, z), device_id_type=MESH
        )
        return _

    lax.fori_loop(0, N_Z - 1, greet_z, 0)
    lax.fori_loop(0, N_LANE - 1, greet_m, 0)
    for a, b in DIRECTIONS:
        pl.semaphore_signal(
            barrier, 1,
            device_id=((g + a + N_GRP) % N_GRP, (t + b + N_TILE) % N_TILE),
            device_id_type=MESH,
        )

    def to_z(stage, source_of, target):
        def send(k, _):
            there = (z + 1 + k) % N_Z
            pltpu.make_async_remote_copy(
                src_ref=source_of(there), dst_ref=target.at[z],
                send_sem=send_sem.at[stage], recv_sem=recv_sem.at[stage],
                device_id=device_at(m, there), device_id_type=MESH,
            ).start()
            return _

        lax.fori_loop(0, N_Z - 1, send, 0)

    def send_m(stage, source, target, there):
        pltpu.make_async_remote_copy(
            src_ref=source, dst_ref=target.at[m],
            send_sem=send_sem.at[stage], recv_sem=recv_sem.at[stage],
            device_id=device_at(there, z), device_id_type=MESH,
        ).start()

    def to_m(stage, source, target):
        def send(k, _):
            send_m(stage, source, target, (m + 1 + k) % N_LANE)
            return _

        lax.fori_loop(0, N_LANE - 1, send, 0)

    def arrived(stage, target, count):
        blocks = target.at[pl.ds(0, count)]
        pltpu.make_async_copy(blocks, blocks, recv_sem.at[stage]).wait()

    def departed(stage, target, count):
        blocks = target.at[pl.ds(0, count)]
        pltpu.make_async_copy(blocks, blocks, send_sem.at[stage]).wait()

    loads[0].wait()
    row = restricted(cells[0, HR:HR + RD, HC:HC + CD], z_lo)
    row_ref[...] = row
    row_in[z] = row

    pl.semaphore_wait(barrier, N_Z - 1 + N_LANE - 1 + len(DIRECTIONS))
    to_z(0, lambda there: row_ref, row_in)

    loads[1].wait()
    row_from = {-1: HR, 0: HR, 1: RD}
    row_to = {-1: HR + RD, 0: HR, 1: 0}
    row_len = {-1: HR, 0: RD, 1: HR}
    col_from = {-1: HC, 0: HC, 1: CD}
    col_to = {-1: HC + CD, 0: HC, 1: 0}
    col_len = {-1: HC, 0: CD, 1: HC}
    halos = []
    for n, (a, b) in enumerate(DIRECTIONS):
        halos.append(pltpu.make_async_remote_copy(
            src_ref=cells.at[:, pl.ds(row_from[a], row_len[a]), pl.ds(col_from[b], col_len[b])],
            dst_ref=cells.at[:, pl.ds(row_to[a], row_len[a]), pl.ds(col_to[b], col_len[b])],
            send_sem=halo_send.at[n], recv_sem=halo_recv.at[n],
            device_id=((g + a + N_GRP) % N_GRP, (t + b + N_TILE) % N_TILE),
            device_id_type=MESH,
        ))
        halos[-1].start()

    arrived(0, row_in, N_Z - 1)
    chunk = jnp.concatenate([row_in[2 * i] + row_in[2 * i + 1] for i in range(4)], axis=0)
    chunk_ref[...] = chunk
    chunk_in[m] = chunk
    to_m(1, chunk_ref, chunk_in)

    for halo in halos:
        halo.wait_recv()
    line = g * RD - HR + lax.broadcasted_iota(jnp.int32, (ER, EC), 0)
    place = t * CD - HC + lanes((ER, EC))
    inside = (line >= 0) & (line < N_GRP * RD) & (place >= 0) & (place < N_TILE * CD)
    right_side = cells[0]
    diagonal = cells[1]
    scale = jnp.where(inside, 0.8 / (6.0 + diagonal), 0.0)
    scale_ref[...] = scale
    smoothed = scale * right_side
    for _ in range(3):
        smoothed = 0.2 * smoothed + scale * (right_side + beside(smoothed))
    smooth[...] = smoothed
    left_over = right_side - (6.0 + diagonal) * smoothed + beside(smoothed)
    part[4:5] = restricted(left_over[HR:HR + RD, HC:HC + CD], z_lo)
    part[5:6] = restricted(diagonal[HR:HR + RD, HC:HC + CD], z_lo)
    part[6:8] = jnp.zeros((2, 128), jnp.float32)

    def transposed(inner, stage, source, target):
        inner = [jnp.broadcast_to(v, (8, 128)) for v in inner]

        def term_of(there):
            for h in range(4):
                where = column(h * 32 + there)
                total = factor[pl.ds(0, 8), where] * inner[0]
                for i in range(1, 8):
                    total = total + factor[pl.ds(8 * i, 8), where] * inner[i]
                source[there, h:h + 1] = jnp.sum(total, axis=0, keepdims=True)

        def step(k, _):
            there = (m + 1 + k) % N_LANE
            term_of(there)
            send_m(stage, source.at[there], target, there)
            return _

        lax.fori_loop(0, N_LANE - 1, step, 0)
        term_of(m)
        target[m] = source[m]

    loads[2].wait()
    arrived(1, chunk_in, N_LANE - 1)
    inner = times_factor(factor, lambda i, s: chunk_in[(s // 4) * 16 + i, s % 4:s % 4 + 1])
    transposed(inner, 2, term, term_in)

    arrived(2, term_in, N_LANE - 1)
    part[0:4] = jnp.sum(term_in[...], axis=0)
    part_in[z] = part[...]
    to_z(3, lambda there: part, part_in)

    arrived(3, part_in, N_Z - 1)
    parts = [part_in[i] for i in range(N_Z)]
    coarse = functools.reduce(jnp.add, [v[0:4] for v in parts])
    rest = jnp.concatenate([parts[2 * i][4:5] + parts[2 * i + 1][4:5] for i in range(4)], axis=0)
    mean_diag = jnp.concatenate(
        [parts[2 * i][5:6] + parts[2 * i + 1][5:6] for i in range(4)], axis=0
    )
    own = rest - 0.5 * (126.0 / 256.0 + mean_diag) * coarse
    fix[...] = jnp.where(
        core == 0,
        jnp.concatenate([coarse, own], axis=0),
        jnp.concatenate([own, coarse], axis=0),
    )
    fix_in[m] = fix[...]
    to_m(4, fix, fix_in)

    arrived(4, fix_in, N_LANE - 1)
    low_rows = lax.broadcasted_iota(jnp.int32, (8, 128), 0) < 4
    field = [jnp.where(low_rows, fix_in[i], fix_in[16 + i]) for i in range(16)]
    around = coarse_neighbours(field)
    for i in range(16):
        own_i = pltpu.roll(jnp.where(low_rows, fix_in[16 + i], fix_in[i]), 4, 0)
        rhs_ref[i] = own_i + (0.5 / 256.0) * around[i]
    inner = times_factor(factor, lambda i, s: rhs_ref[i, s:s + 1])
    transposed(inner, 5, term_b, term_b_in)

    def coarse_rows(b):
        tt = t + b
        ok_t = (tt >= 0) & (tt < N_TILE)
        tt = (tt + N_TILE) % N_TILE
        rows = []
        for a, i_hi in ((-1, 1), (0, 0), (0, 1), (1, 0)):
            gg = g + a
            ok = ok_t & (gg >= 0) & (gg < N_GRP)
            gg = (gg + N_GRP) % N_GRP
            row = fix_in[(gg % 2) * 16 + tt // 2, pl.ds((gg % 2) * 4 + gg // 2, 1)]
            rows.append(quarter(row, tt % 2, i_hi, ok))
        return jnp.concatenate(rows + [jnp.zeros((4, 128), jnp.float32)], axis=0)

    lane8 = lanes((8, 128))
    at_left = jnp.sum(jnp.where(lane8 % 32 == 31, coarse_rows(-1), 0.0), axis=1, keepdims=True)
    at_right = jnp.sum(jnp.where(lane8 % 32 == 0, coarse_rows(1), 0.0), axis=1, keepdims=True)
    wide = 0.5 * jnp.concatenate(
        [
            jnp.broadcast_to(at_left, (8, HC)),
            spread_columns(coarse_rows(0)),
            jnp.broadcast_to(at_right, (8, HC)),
        ],
        axis=1,
    )
    fine = jnp.concatenate(
        [
            jnp.broadcast_to(wide[0:1], (HR, EC)),
            jnp.broadcast_to(wide[1:2], (FAC, EC)),
            jnp.broadcast_to(wide[2:3], (FAC, EC)),
            jnp.broadcast_to(wide[3:4], (HR, EC)),
        ],
        axis=0,
    )
    iterate = smooth[...] + fine
    residual = cells[0] - (6.0 + cells[1]) * iterate + beside(iterate)
    scale = scale_ref[...]
    smoothed = scale * residual
    for _ in range(3):
        smoothed = 0.2 * smoothed + scale * (residual + beside(smoothed))
    result[...] = (iterate + smoothed)[HR:HR + RD, HC:HC + CD]

    arrived(5, term_b_in, N_LANE - 1)
    summed = jnp.sum(term_b_in[...], axis=0)
    for i in range(4):
        last[i] = summed[i:i + 1]
    last_in[z] = last[z_hi]
    to_z(6, lambda there: last.at[there // 2], last_in)
    arrived(6, last_in, N_Z - 1)
    row = functools.reduce(jnp.add, [last_in[i] for i in range(N_Z)])
    pair = jnp.concatenate(
        [quarter(row, z_lo, 0, True), quarter(row, z_lo, 1, True), jnp.zeros((6, 128), jnp.float32)],
        axis=0,
    )
    pair = 0.5 * spread_columns(pair)
    out_ref[:FAC] = result[:FAC] + pair[0:1]
    out_ref[FAC:] = result[FAC:] + pair[1:2]

    for halo in halos:
        halo.wait_send()
    departed(0, row_in, N_Z - 1)
    departed(1, chunk_in, N_LANE - 1)
    departed(2, term_in, N_LANE - 1)
    departed(3, part_in, N_Z - 1)
    departed(4, fix_in, N_LANE - 1)
    departed(5, term_b_in, N_LANE - 1)
    departed(6, last_in, N_Z - 1)


def shards(right_side, diagonal, inverse_factor):
    f32 = jnp.float32
    return pl.pallas_call(
        kernel,
        out_shape=jax.ShapeDtypeStruct((RD, CD), f32),
        in_specs=[pl.BlockSpec(memory_space=pl.ANY)] * 3,
        out_specs=pl.BlockSpec(memory_space=pltpu.VMEM),
        scratch_shapes=[
            pltpu.VMEM((2, ER, EC), f32),
            pltpu.VMEM((CO, N_GRP * N_TILE * CO), f32),
            pltpu.VMEM((ER, EC), f32),
            pltpu.VMEM((ER, EC), f32),
            pltpu.VMEM((RD, CD), f32),
            pltpu.VMEM((1, 128), f32),
            pltpu.VMEM((N_Z, 1, 128), f32),
            pltpu.VMEM((4, 128), f32),
            pltpu.VMEM((N_LANE, 4, 128), f32),
            pltpu.VMEM((N_LANE, 4, 128), f32),
            pltpu.VMEM((N_LANE, 4, 128), f32),
            pltpu.VMEM((8, 128), f32),
            pltpu.VMEM((N_Z, 8, 128), f32),
            pltpu.VMEM((8, 128), f32),
            pltpu.VMEM((N_LANE, 8, 128), f32),
            pltpu.VMEM((16, 8, 128), f32),
            pltpu.VMEM((N_LANE, 4, 128), f32),
            pltpu.VMEM((N_LANE, 4, 128), f32),
            pltpu.VMEM((4, 1, 128), f32),
            pltpu.VMEM((N_Z, 1, 128), f32),
            pltpu.SemaphoreType.DMA((3,)),
            pltpu.SemaphoreType.DMA((len(DIRECTIONS),)),
            pltpu.SemaphoreType.DMA((len(DIRECTIONS),)),
            pltpu.SemaphoreType.DMA((7,)),
            pltpu.SemaphoreType.DMA((7,)),
        ],
        compiler_params=pltpu.CompilerParams(
            collective_id=0, has_side_effects=True, vmem_limit_bytes=24 * 1024 * 1024
        ),
    )(right_side, diagonal, inverse_factor)


def solution(mesh):
    placed = (P("grp", "tile"), P("grp", "tile"), P(("grp", "tile"), None))
    return jax.shard_map(
        shards, mesh=mesh, in_specs=placed, out_specs=P("grp", "tile"), check_vma=False
    )
```

time: 1100 us -> 51.8 us (0.05)
  waiting for transfers between devices: 965 us -> 0 us
  starting transfers between devices: 89.7 us -> 0 us
  Pallas kernels: 0 us -> 47.1 us
  matrix products: 16.9 us -> 0 us
  between operations: 13.7 us -> 0.01 us
    unnamed x6 -> x0, waiting for transfers between devices: 478 us -> none
    psum x2 -> x0, waiting for transfers between devices: 468 us -> none  [shards(): summed = lax.psum(whole_term, ('grp', 'tile'))]
    ppermute x28 -> x0, starting transfers between devices: 89.6 us -> none  [the longest x14 63.7 us: extended(): lax.ppermute(lax.slice_in_dim(block, block.shape[dim] - width, None, axis...]
    pallas_call x0 -> x1, Pallas kernels: none -> 47.1 us  [shards(): pl.pallas_call(kernel, out_shape=jax.ShapeDtypeStruct((RD, CD), f32), in_...]
    ppermute x28 -> x0, waiting for transfers between devices: 18.5 us -> none  [the longest x14 15.9 us: extended(): lax.ppermute(lax.slice_in_dim(block, 0, width, axis=dim), axis, backward)]
    dot_general x4 -> x0, matrix products: 16.9 us -> none  [the longest x2 11.4 us: shards(): jnp.dot(inverse_factor, lax.all_gather(coarse_rhs, ('grp', 'tile'), axis=...]
  transfers between devices with their start and end apart: 32 -> 0, of which waited for: 13 -> 0; matrix products, arithmetic and copies ran while one was open for 2% -> 0% of each run, Pallas kernels for 0% -> 0%
where the time goes in v1:
time: 51.8 us; the launch traced here: 51.6 us
  Pallas kernels  47.1 us (91%)
  local copies, waits for them, and re-layouts  4.5 us (9%)
    pallas_call x1, Pallas kernels, shards(): pl.pallas_call(kernel, out_shape=jax.ShapeDtypeStruct((RD, CD), f32), in_...  47.1 us
    unnamed x7, local copies, waits for them, and re-layouts  4.5 us

profile of v1, /device:TPU:1, one launch (start us, length us, event | category | flops | bytes accessed | tf_op | source)
XLA Modules:
  0.0 51.6 jit_solution(8321708621439065923)
XLA Ops:
  0.0 0.0 copy-start
  0.0 2.2 %copy-done = f32[64,16384]{1,0:T(8,128)S(1)} copy-done((f32[64,16384]{1,0:T(8,128)S(1)}, f32[64,16384]{1,0:T(8,128)}, u32[]{:S(2)}) %copy-start) | copy-done | bytes 4194328
  2.2 0.0 copy-start.1
  2.2 0.8 %copy-done.1 = f32[32,512]{1,0:T(8,128)S(1)} copy-done((f32[32,512]{1,0:T(8,128)S(1)}, f32[32,512]{1,0:T(8,128)}, u32[]{:S(2)}) %copy-start.1) | copy-done | bytes 65560
  3.0 0.0 copy-start.2
  3.0 0.8 %copy-done.2 = f32[32,512]{1,0:T(8,128)S(1)} copy-done((f32[32,512]{1,0:T(8,128)S(1)}, f32[32,512]{1,0:T(8,128)}, u32[]{:S(2)}) %copy-start.2) | copy-done | bytes 65560
  3.9 47.1 %shard_map.37 = f32[32,512]{1,0:T(8,128)S(1)} custom-call(f32[32,512]{1,0:T(8,128)S(1)} %copy-done.1, f32[32,512]{1,0:T(8,128)S(1)} %copy-done.2, f32[64,16384]{1,0:T(8,128)S(1)} %copy-done), custom_call_target="tpu_custom_call" | custom-call | tf_op jit(solution)/shard_map/pallas_call | solution.py:364
  51.0 0.6 %copy.5 = f32[32,512]{1,0:T(8,128)} copy(f32[32,512]{1,0:T(8,128)S(1)} %shard_map.37) | data formatting | bytes 131072
Async XLA Ops:
  0.0 2.2 %copy-start = (f32[64,16384]{1,0:T(8,128)S(1)}, f32[64,16384]{1,0:T(8,128)}, u32[]{:S(2)}) copy-start(f32[64,16384]{1,0:T(8,128)} %factor_ref.1) | copy-start | bytes 12582916
  2.2 0.8 %copy-start.1 = (f32[32,512]{1,0:T(8,128)S(1)}, f32[32,512]{1,0:T(8,128)}, u32[]{:S(2)}) copy-start(f32[32,512]{1,0:T(8,128)} %right_ref.1) | copy-start | bytes 196612
  3.0 0.8 %copy-start.2 = (f32[32,512]{1,0:T(8,128)S(1)}, f32[32,512]{1,0:T(8,128)}, u32[]{:S(2)}) copy-start(f32[32,512]{1,0:T(8,128)} %diag_ref.1) | copy-start | bytes 196612

commit v2 on v1

--- a/solution.py
+++ b/solution.py
@@ -15,11 +15,24 @@
 ER, EC = RD + 2 * HR, CD + 2 * HC
 CO = 64
 N_LANE, N_Z = 32, 8
+OFFSETS = sorted(
+    ((a, b) for a in range(4) for b in range(4)),
+    key=lambda o: -(min(o[0], 4 - o[0]) + min(o[1], 4 - o[1])),
+)
+Z_OFFSETS = (4, 3, 5, 2, 6, 1, 7)
+HOPS = 5
 DIRECTIONS = [(a, b) for a in (-1, 0, 1) for b in (-1, 0, 1) if (a, b) != (0, 0)]
 
 
-def device_at(m, z):
-    return ((z // 2) * 2 + m // 16, (m % 16) * 2 + z % 2)
+def hops(offset):
+    return min(offset[0], 4 - offset[0]) + min(offset[1], 4 - offset[1])
+
+
+def pick(k, values):
+    out = jnp.int32(values[-1])
+    for i, value in enumerate(values[:-1]):
+        out = jnp.where(k == i, jnp.int32(value), out)
+    return out
 
 
 def beside(field):
@@ -92,8 +105,9 @@
     return pl.ds(pl.multiple_of(tile * 128, 128), 128)
 
 
-def times_factor(factor, row_of):
-    def step(xy, totals):
+def add_products(factor, totals, count, place_of, row_of):
+    def step(k, totals):
+        xy = place_of(k)
         totals = list(totals)
         for s in range(8):
             row = row_of(xy, s)
@@ -102,9 +116,9 @@
                 totals[i] = totals[i] + factor[pl.ds(8 * i, 8), where] * row
         return tuple(totals)
 
-    zero = jnp.zeros((8, 128), jnp.float32)
-    totals = lax.fori_loop(0, 16, step, (zero,) * 8)
-    return [jnp.sum(v, axis=1, keepdims=True) for v in totals]
+    if count == 1:
+        return step(0, totals)
+    return lax.fori_loop(0, count, step, totals)
 
 
 def kernel(
@@ -112,12 +126,32 @@
     cells, factor, smooth, scale_ref, result,
     row_ref, row_in, chunk_ref, chunk_in, term, term_in, part, part_in,
     fix, fix_in, rhs_ref, term_b, term_b_in, last, last_in,
-    load_sem, halo_send, halo_recv, send_sem, recv_sem,
+    load_sem, halo_send, halo_recv, send_sem, recv_sem, chunk_sem, fix_sem,
 ):
     g, t = lax.axis_index("grp"), lax.axis_index("tile")
-    z_hi, core, xy, z_lo = g // 2, g % 2, t // 2, t % 2
+    z_hi, core = lax.div(g, 2), lax.rem(g, 2)
+    xy, z_lo = lax.div(t, 2), lax.rem(t, 2)
+    x, y = lax.div(xy, 4), lax.rem(xy, 4)
     m, z = core * 16 + xy, z_hi * 2 + z_lo
     rows_in, cols_in = pl.ds(HR, RD), pl.ds(HC, CD)
+    xs = [lax.rem(x + a, 4) for a in range(4)]
+    ys = [lax.rem(y + b, 4) for b in range(4)]
+    zs = [lax.rem(z + c, 8) for c in range(8)]
+    mates = [
+        (hops(o), (z_hi * 2 + c, xs[o[0]] * 8 + ys[o[1]] * 2 + z_lo))
+        for o in OFFSETS[:-1] for c in range(2)
+    ]
+    mates.append((0, (z_hi * 2 + 1 - core, t)))
+    column_mates = [
+        (zs[c], (lax.div(zs[c], 2) * 2 + core, xy * 2 + lax.rem(zs[c], 2))) for c in Z_OFFSETS
+    ]
+    beside_here = [
+        (lax.rem(g + a + N_GRP, N_GRP), lax.rem(t + b + N_TILE, N_TILE)) for a, b in DIRECTIONS
+    ]
+
+    barrier = pltpu.get_barrier_semaphore()
+    for device in [d for _, d in column_mates] + [d for _, d in mates] + beside_here:
+        pl.semaphore_signal(barrier, 1, device_id=device, device_id_type=MESH)
 
     loads = [
         pltpu.make_async_copy(right_ref, cells.at[0, rows_in, cols_in], load_sem.at[0]),
@@ -127,58 +161,28 @@
     for load in loads:
         load.start()
 
-    barrier = pltpu.get_barrier_semaphore()
-
-    def greet_z(k, _):
-        pl.semaphore_signal(
-            barrier, 1, device_id=device_at(m, (z + 1 + k) % N_Z), device_id_type=MESH
-        )
-        return _
-
-    def greet_m(k, _):
-        pl.semaphore_signal(
-            barrier, 1, device_id=device_at((m + 1 + k) % N_LANE, z), device_id_type=MESH
-        )
-        return _
-
-    lax.fori_loop(0, N_Z - 1, greet_z, 0)
-    lax.fori_loop(0, N_LANE - 1, greet_m, 0)
-    for a, b in DIRECTIONS:
-        pl.semaphore_signal(
-            barrier, 1,
-            device_id=((g + a + N_GRP) % N_GRP, (t + b + N_TILE) % N_TILE),
-            device_id_type=MESH,
-        )
-
     def to_z(stage, source_of, target):
-        def send(k, _):
-            there = (z + 1 + k) % N_Z
+        for there, device in column_mates:
             pltpu.make_async_remote_copy(
                 src_ref=source_of(there), dst_ref=target.at[z],
                 send_sem=send_sem.at[stage], recv_sem=recv_sem.at[stage],
-                device_id=device_at(m, there), device_id_type=MESH,
+                device_id=device, device_id_type=MESH,
             ).start()
-            return _
-
-        lax.fori_loop(0, N_Z - 1, send, 0)
-
-    def send_m(stage, source, target, there):
-        pltpu.make_async_remote_copy(
-            src_ref=source, dst_ref=target.at[m],
-            send_sem=send_sem.at[stage], recv_sem=recv_sem.at[stage],
-            device_id=device_at(there, z), device_id_type=MESH,
-        ).start()
-
-    def to_m(stage, source, target):
-        def send(k, _):
-            send_m(stage, source, target, (m + 1 + k) % N_LANE)
-            return _
-
-        lax.fori_loop(0, N_LANE - 1, send, 0)
-
-    def arrived(stage, target, count):
+
+    def to_m(stage, source, target, near):
+        for distance, device in mates:
+            pltpu.make_async_remote_copy(
+                src_ref=source, dst_ref=target.at[m],
+                send_sem=send_sem.at[stage], recv_sem=near.at[distance],
+                device_id=device, device_id_type=MESH,
+            ).start()
+
+    def arrived(sem, target, count):
         blocks = target.at[pl.ds(0, count)]
-        pltpu.make_async_copy(blocks, blocks, recv_sem.at[stage]).wait()
+        pltpu.make_async_copy(blocks, blocks, sem).wait()
+
+    def arrived_from(near, target, distance):
+        arrived(near.at[distance], target, sum(d == distance for d, _ in mates))
 
     def departed(stage, target, count):
         blocks = target.at[pl.ds(0, count)]
@@ -205,16 +209,16 @@
             src_ref=cells.at[:, pl.ds(row_from[a], row_len[a]), pl.ds(col_from[b], col_len[b])],
             dst_ref=cells.at[:, pl.ds(row_to[a], row_len[a]), pl.ds(col_to[b], col_len[b])],
             send_sem=halo_send.at[n], recv_sem=halo_recv.at[n],
-            device_id=((g + a + N_GRP) % N_GRP, (t + b + N_TILE) % N_TILE),
+            device_id=beside_here[n],
             device_id_type=MESH,
         ))
         halos[-1].start()
 
-    arrived(0, row_in, N_Z - 1)
+    arrived(recv_sem.at[0], row_in, N_Z - 1)
     chunk = jnp.concatenate([row_in[2 * i] + row_in[2 * i + 1] for i in range(4)], axis=0)
     chunk_ref[...] = chunk
     chunk_in[m] = chunk
-    to_m(1, chunk_ref, chunk_in)
+    to_m(1, chunk_ref, chunk_in, chunk_sem)
 
     for halo in halos:
         halo.wait_recv()
@@ -245,27 +249,54 @@
                     total = total + factor[pl.ds(8 * i, 8), where] * inner[i]
                 source[there, h:h + 1] = jnp.sum(total, axis=0, keepdims=True)
 
+        def send(there, device):
+            pltpu.make_async_remote_copy(
+                src_ref=source.at[there], dst_ref=target.at[m],
+                send_sem=send_sem.at[stage], recv_sem=recv_sem.at[stage],
+                device_id=device, device_id_type=MESH,
+            ).start()
+
         def step(k, _):
-            there = (m + 1 + k) % N_LANE
-            term_of(there)
-            send_m(stage, source.at[there], target, there)
+            xx = lax.rem(x + pick(k, [o[0] for o in OFFSETS]), 4)
+            yy = lax.rem(y + pick(k, [o[1] for o in OFFSETS]), 4)
+            for c in range(2):
+                there = c * 16 + xx * 4 + yy
+                term_of(there)
+                send(there, (z_hi * 2 + c, xx * 8 + yy * 2 + z_lo))
             return _
 
-        lax.fori_loop(0, N_LANE - 1, step, 0)
+        lax.fori_loop(0, len(OFFSETS) - 1, step, 0)
+        other = (1 - core) * 16 + xy
+        term_of(other)
+        send(other, (z_hi * 2 + 1 - core, t))
         term_of(m)
         target[m] = source[m]
 
+    none = (jnp.zeros((8, 128), jnp.float32),) * 8
+
+    def summed_lanes(totals):
+        return [jnp.sum(v, axis=1, keepdims=True) for v in totals]
+
     loads[2].wait()
-    arrived(1, chunk_in, N_LANE - 1)
-    inner = times_factor(factor, lambda i, s: chunk_in[(s // 4) * 16 + i, s % 4:s % 4 + 1])
-    transposed(inner, 2, term, term_in)
-
-    arrived(2, term_in, N_LANE - 1)
+    totals = none
+    for group in ((0, 1, 2), (3,), (4,)):
+        for distance in group:
+            arrived_from(chunk_sem, chunk_in, distance)
+        members = [o for o in OFFSETS if hops(o) in group]
+        totals = add_products(
+            factor, totals, len(members),
+            lambda k: (lax.rem(x + pick(k, [o[0] for o in members]), 4) * 4
+                       + lax.rem(y + pick(k, [o[1] for o in members]), 4)),
+            lambda i, s: chunk_in[(s // 4) * 16 + i, s % 4:s % 4 + 1],
+        )
+    transposed(summed_lanes(totals), 2, term, term_in)
+
+    arrived(recv_sem.at[2], term_in, N_LANE - 1)
     part[0:4] = jnp.sum(term_in[...], axis=0)
     part_in[z] = part[...]
     to_z(3, lambda there: part, part_in)
 
-    arrived(3, part_in, N_Z - 1)
+    arrived(recv_sem.at[3], part_in, N_Z - 1)
     parts = [part_in[i] for i in range(N_Z)]
     coarse = functools.reduce(jnp.add, [v[0:4] for v in parts])
     rest = jnp.concatenate([parts[2 * i][4:5] + parts[2 * i + 1][4:5] for i in range(4)], axis=0)
@@ -279,17 +310,18 @@
         jnp.concatenate([own, coarse], axis=0),
     )
     fix_in[m] = fix[...]
-    to_m(4, fix, fix_in)
-
-    arrived(4, fix_in, N_LANE - 1)
+    to_m(4, fix, fix_in, fix_sem)
+
+    for distance in range(HOPS):
+        arrived_from(fix_sem, fix_in, distance)
     low_rows = lax.broadcasted_iota(jnp.int32, (8, 128), 0) < 4
     field = [jnp.where(low_rows, fix_in[i], fix_in[16 + i]) for i in range(16)]
     around = coarse_neighbours(field)
     for i in range(16):
         own_i = pltpu.roll(jnp.where(low_rows, fix_in[16 + i], fix_in[i]), 4, 0)
         rhs_ref[i] = own_i + (0.5 / 256.0) * around[i]
-    inner = times_factor(factor, lambda i, s: rhs_ref[i, s:s + 1])
-    transposed(inner, 5, term_b, term_b_in)
+    totals = add_products(factor, none, 16, lambda k: k, lambda i, s: rhs_ref[i, s:s + 1])
+    transposed(summed_lanes(totals), 5, term_b, term_b_in)
 
     def coarse_rows(b):
         tt = t + b
@@ -332,13 +364,13 @@
         smoothed = 0.2 * smoothed + scale * (residual + beside(smoothed))
     result[...] = (iterate + smoothed)[HR:HR + RD, HC:HC + CD]
 
-    arrived(5, term_b_in, N_LANE - 1)
+    arrived(recv_sem.at[5], term_b_in, N_LANE - 1)
     summed = jnp.sum(term_b_in[...], axis=0)
     for i in range(4):
         last[i] = summed[i:i + 1]
     last_in[z] = last[z_hi]
-    to_z(6, lambda there: last.at[there // 2], last_in)
-    arrived(6, last_in, N_Z - 1)
+    to_z(6, lambda there: last.at[lax.div(there, 2)], last_in)
+    arrived(recv_sem.at[6], last_in, N_Z - 1)
     row = functools.reduce(jnp.add, [last_in[i] for i in range(N_Z)])
     pair = jnp.concatenate(
         [quarter(row, z_lo, 0, True), quarter(row, z_lo, 1, True), jnp.zeros((6, 128), jnp.float32)],
@@ -364,7 +396,7 @@
     return pl.pallas_call(
         kernel,
         out_shape=jax.ShapeDtypeStruct((RD, CD), f32),
-        in_specs=[pl.BlockSpec(memory_space=pl.ANY)] * 3,
+        in_specs=[pl.BlockSpec(memory_space=pltpu.HBM)] * 3,
         out_specs=pl.BlockSpec(memory_space=pltpu.VMEM),
         scratch_shapes=[
             pltpu.VMEM((2, ER, EC), f32),
@@ -392,9 +424,11 @@
             pltpu.SemaphoreType.DMA((len(DIRECTIONS),)),
             pltpu.SemaphoreType.DMA((7,)),
             pltpu.SemaphoreType.DMA((7,)),
+            pltpu.SemaphoreType.DMA((HOPS,)),
+            pltpu.SemaphoreType.DMA((HOPS,)),
         ],
         compiler_params=pltpu.CompilerParams(
-            collective_id=0, has_side_effects=True, vmem_limit_bytes=24 * 1024 * 1024
+            collective_id=0, has_side_effects=True, vmem_limit_bytes=60 * 1024 * 1024
         ),
     )(right_side, diagonal, inverse_factor)
 

time: 51.8 us -> 47.3 us (0.913)
  local copies, waits for them, and re-layouts: 4.5 us -> 1.47 us
  Pallas kernels: 47.1 us -> 45.7 us
    unnamed x7 -> x1, local copies, waits for them, and re-layouts: 4.5 us -> 1.47 us
    pallas_call x1, Pallas kernels: 47.1 us -> 45.7 us  [shards(): pl.pallas_call(kernel, out_shape=jax.ShapeDtypeStruct((RD, CD), f32), in_...]
where the time goes in v2:
time: 47.3 us; the launch traced here: 47.2 us
  Pallas kernels  45.7 us (97%)
  local copies, waits for them, and re-layouts  1.47 us (3%)
    pallas_call x1, Pallas kernels, shards(): pl.pallas_call(kernel, out_shape=jax.ShapeDtypeStruct((RD, CD), f32), in_...  45.7 us
    unnamed x1, local copies, waits for them, and re-layouts  1.47 us

profile of v2, /device:TPU:1, one launch (start us, length us, event | category | flops | bytes accessed | tf_op | source)
XLA Modules:
  0.0 47.2 jit_solution(7202522954469285875)
XLA Ops:
  0.0 45.7 %shard_map.37 = f32[32,512]{1,0:T(8,128)} custom-call(f32[32,512]{1,0:T(8,128)} %right_ref.1, f32[32,512]{1,0:T(8,128)} %diag_ref.1, f32[64,16384]{1,0:T(8,128)} %factor_ref.1), custom_call_target="tpu_custom_call" | custom-call | tf_op jit(solution)/shard_map/pallas_call | solution.py:396
  45.7 1.5 %copy.5 = f32[32,512]{1,0:T(8,128)} copy(f32[32,512]{1,0:T(8,128)} %shard_map.37) | data formatting | bytes 131072

commit v3 on v2

--- a/solution.py
+++ b/solution.py
@@ -125,8 +125,8 @@
     right_ref, diag_ref, factor_ref, out_ref,
     cells, factor, smooth, scale_ref, result,
     row_ref, row_in, chunk_ref, chunk_in, term, term_in, part, part_in,
-    fix, fix_in, rhs_ref, term_b, term_b_in, last, last_in,
-    load_sem, halo_send, halo_recv, send_sem, recv_sem, chunk_sem, fix_sem,
+    fix, fix_in, rhs_ref, last, last_in,
+    load_sem, halo_send, halo_recv, send_sem, recv_sem, chunk_sem, fix_sem, last_sem,
 ):
     g, t = lax.axis_index("grp"), lax.axis_index("tile")
     z_hi, core = lax.div(g, 2), lax.rem(g, 2)
@@ -238,7 +238,7 @@
     part[5:6] = restricted(diagonal[HR:HR + RD, HC:HC + CD], z_lo)
     part[6:8] = jnp.zeros((2, 128), jnp.float32)
 
-    def transposed(inner, stage, source, target):
+    def transposed(inner, store, send):
         inner = [jnp.broadcast_to(v, (8, 128)) for v in inner]
 
         def term_of(there):
@@ -247,30 +247,44 @@
                 total = factor[pl.ds(0, 8), where] * inner[0]
                 for i in range(1, 8):
                     total = total + factor[pl.ds(8 * i, 8), where] * inner[i]
-                source[there, h:h + 1] = jnp.sum(total, axis=0, keepdims=True)
-
-        def send(there, device):
-            pltpu.make_async_remote_copy(
-                src_ref=source.at[there], dst_ref=target.at[m],
-                send_sem=send_sem.at[stage], recv_sem=recv_sem.at[stage],
-                device_id=device, device_id_type=MESH,
-            ).start()
+                store(there, h, jnp.sum(total, axis=0, keepdims=True))
 
         def step(k, _):
             xx = lax.rem(x + pick(k, [o[0] for o in OFFSETS]), 4)
             yy = lax.rem(y + pick(k, [o[1] for o in OFFSETS]), 4)
             for c in range(2):
-                there = c * 16 + xx * 4 + yy
-                term_of(there)
-                send(there, (z_hi * 2 + c, xx * 8 + yy * 2 + z_lo))
+                term_of(c * 16 + xx * 4 + yy)
+                send(c, xx * 4 + yy, k)
             return _
 
         lax.fori_loop(0, len(OFFSETS) - 1, step, 0)
-        other = (1 - core) * 16 + xy
-        term_of(other)
-        send(other, (z_hi * 2 + 1 - core, t))
+        term_of((1 - core) * 16 + xy)
+        send(1 - core, xy, len(OFFSETS) - 1)
         term_of(m)
-        target[m] = source[m]
+
+    def store_term(there, h, row):
+        term[there, h:h + 1] = row
+
+    def send_term(c, there, k):
+        pltpu.make_async_remote_copy(
+            src_ref=term.at[c * 16 + there], dst_ref=term_in.at[m],
+            send_sem=send_sem.at[2], recv_sem=recv_sem.at[2],
+            device_id=(z_hi * 2 + c, there * 2 + z_lo), device_id_type=MESH,
+        ).start()
+
+    def store_last(there, h, row):
+        last[there, h] = row
+
+    def send_last(c, there, k, places=(*Z_OFFSETS, 0)):
+        distance = pick(k, [hops(o) for o in OFFSETS]) if k is not len(OFFSETS) - 1 else 0
+        for i, o in enumerate(places):
+            half = lax.div(zs[o], 2)
+            pltpu.make_async_remote_copy(
+                src_ref=last.at[c * 16 + there, half],
+                dst_ref=last_in.at[(k * 2 + core) * N_Z + i],
+                send_sem=send_sem.at[4], recv_sem=last_sem.at[distance],
+                device_id=(half * 2 + c, there * 2 + lax.rem(zs[o], 2)), device_id_type=MESH,
+            ).start()
 
     none = (jnp.zeros((8, 128), jnp.float32),) * 8
 
@@ -289,7 +303,8 @@
                        + lax.rem(y + pick(k, [o[1] for o in members]), 4)),
             lambda i, s: chunk_in[(s // 4) * 16 + i, s % 4:s % 4 + 1],
         )
-    transposed(summed_lanes(totals), 2, term, term_in)
+    transposed(summed_lanes(totals), store_term, send_term)
+    term_in[m] = term[m]
 
     arrived(recv_sem.at[2], term_in, N_LANE - 1)
     part[0:4] = jnp.sum(term_in[...], axis=0)
@@ -310,7 +325,7 @@
         jnp.concatenate([own, coarse], axis=0),
     )
     fix_in[m] = fix[...]
-    to_m(4, fix, fix_in, fix_sem)
+    to_m(5, fix, fix_in, fix_sem)
 
     for distance in range(HOPS):
         arrived_from(fix_sem, fix_in, distance)
@@ -321,7 +336,9 @@
         own_i = pltpu.roll(jnp.where(low_rows, fix_in[16 + i], fix_in[i]), 4, 0)
         rhs_ref[i] = own_i + (0.5 / 256.0) * around[i]
     totals = add_products(factor, none, 16, lambda k: k, lambda i, s: rhs_ref[i, s:s + 1])
-    transposed(summed_lanes(totals), 5, term_b, term_b_in)
+    transposed(summed_lanes(totals), store_last, send_last)
+    send_last(core, xy, len(OFFSETS) - 1, Z_OFFSETS)
+    last_in[((len(OFFSETS) - 1) * 2 + core) * N_Z + N_Z - 1] = last[m, z_hi]
 
     def coarse_rows(b):
         tt = t + b
@@ -364,14 +381,12 @@
         smoothed = 0.2 * smoothed + scale * (residual + beside(smoothed))
     result[...] = (iterate + smoothed)[HR:HR + RD, HC:HC + CD]
 
-    arrived(recv_sem.at[5], term_b_in, N_LANE - 1)
-    summed = jnp.sum(term_b_in[...], axis=0)
-    for i in range(4):
-        last[i] = summed[i:i + 1]
-    last_in[z] = last[z_hi]
-    to_z(6, lambda there: last.at[lax.div(there, 2)], last_in)
-    arrived(recv_sem.at[6], last_in, N_Z - 1)
-    row = functools.reduce(jnp.add, [last_in[i] for i in range(N_Z)])
+    row = jnp.zeros((1, 128), jnp.float32)
+    for distance in range(HOPS):
+        places = [k for k, o in enumerate(OFFSETS) if hops(o) == distance]
+        first, count = places[0] * 2 * N_Z, len(places) * 2 * N_Z
+        arrived(last_sem.at[distance], last_in, count - (distance == 0))
+        row = row + jnp.sum(last_in[first:first + count], axis=0)
     pair = jnp.concatenate(
         [quarter(row, z_lo, 0, True), quarter(row, z_lo, 1, True), jnp.zeros((6, 128), jnp.float32)],
         axis=0,
@@ -386,9 +401,8 @@
     departed(1, chunk_in, N_LANE - 1)
     departed(2, term_in, N_LANE - 1)
     departed(3, part_in, N_Z - 1)
-    departed(4, fix_in, N_LANE - 1)
-    departed(5, term_b_in, N_LANE - 1)
-    departed(6, last_in, N_Z - 1)
+    departed(5, fix_in, N_LANE - 1)
+    departed(4, last_in, N_GRP * N_TILE - 1)
 
 
 def shards(right_side, diagonal, inverse_factor):
@@ -415,20 +429,19 @@
             pltpu.VMEM((8, 128), f32),
             pltpu.VMEM((N_LANE, 8, 128), f32),
             pltpu.VMEM((16, 8, 128), f32),
-            pltpu.VMEM((N_LANE, 4, 128), f32),
-            pltpu.VMEM((N_LANE, 4, 128), f32),
-            pltpu.VMEM((4, 1, 128), f32),
-            pltpu.VMEM((N_Z, 1, 128), f32),
+            pltpu.VMEM((N_LANE, 4, 1, 128), f32),
+            pltpu.VMEM((N_GRP * N_TILE, 1, 128), f32),
             pltpu.SemaphoreType.DMA((3,)),
             pltpu.SemaphoreType.DMA((len(DIRECTIONS),)),
             pltpu.SemaphoreType.DMA((len(DIRECTIONS),)),
-            pltpu.SemaphoreType.DMA((7,)),
-            pltpu.SemaphoreType.DMA((7,)),
+            pltpu.SemaphoreType.DMA((6,)),
+            pltpu.SemaphoreType.DMA((4,)),
+            pltpu.SemaphoreType.DMA((HOPS,)),
             pltpu.SemaphoreType.DMA((HOPS,)),
             pltpu.SemaphoreType.DMA((HOPS,)),
         ],
         compiler_params=pltpu.CompilerParams(
-            collective_id=0, has_side_effects=True, vmem_limit_bytes=60 * 1024 * 1024
+            collective_id=0, has_side_effects=True, vmem_limit_bytes=55160 * 1024
         ),
     )(right_side, diagonal, inverse_factor)
 

time: 47.3 us -> 45.1 us (0.953)
  Pallas kernels: 45.7 us -> 44.4 us
  local copies, waits for them, and re-layouts: 1.47 us -> 0.63 us
    pallas_call x1, Pallas kernels: 45.7 us -> 44.4 us  [shards(): pl.pallas_call(kernel, out_shape=jax.ShapeDtypeStruct((RD, CD), f32), in_...]
    unnamed x1, local copies, waits for them, and re-layouts: 1.47 us -> 0.63 us
where the time goes in v3:
time: 45.1 us; the launch traced here: 45 us
  Pallas kernels  44.4 us (98%)
  local copies, waits for them, and re-layouts  0.63 us (1%)
    pallas_call x1, Pallas kernels, shards(): pl.pallas_call(kernel, out_shape=jax.ShapeDtypeStruct((RD, CD), f32), in_...  44.4 us

profile of v3, /device:TPU:1, one launch (start us, length us, event | category | flops | bytes accessed | tf_op | source)
XLA Modules:
  0.0 45.0 jit_solution(270158338784016059)
XLA Ops:
  0.0 44.4 %shard_map.37 = f32[32,512]{1,0:T(8,128)S(1)} custom-call(f32[32,512]{1,0:T(8,128)} %right_ref.1, f32[32,512]{1,0:T(8,128)} %diag_ref.1, f32[64,16384]{1,0:T(8,128)} %factor_ref.1), custom_call_target="tpu_custom_call" | custom-call | tf_op jit(solution)/shard_map/pallas_call | solution.py:410
  44.4 0.6 %copy.5 = f32[32,512]{1,0:T(8,128)} copy(f32[32,512]{1,0:T(8,128)S(1)} %shard_map.37) | data formatting | bytes 131072

commit v4 on v3

--- a/solution.py
+++ b/solution.py
@@ -20,6 +20,7 @@
     key=lambda o: -(min(o[0], 4 - o[0]) + min(o[1], 4 - o[1])),
 )
 Z_OFFSETS = (4, 3, 5, 2, 6, 1, 7)
+GROUP = 2
 HOPS = 5
 DIRECTIONS = [(a, b) for a in (-1, 0, 1) for b in (-1, 0, 1) if (a, b) != (0, 0)]
 
@@ -118,7 +119,7 @@
 
     if count == 1:
         return step(0, totals)
-    return lax.fori_loop(0, count, step, totals)
+    return lax.fori_loop(0, count, step, totals, unroll=4)
 
 
 def kernel(
@@ -244,20 +245,32 @@
         def term_of(there):
             for h in range(4):
                 where = column(h * 32 + there)
-                total = factor[pl.ds(0, 8), where] * inner[0]
-                for i in range(1, 8):
-                    total = total + factor[pl.ds(8 * i, 8), where] * inner[i]
-                store(there, h, jnp.sum(total, axis=0, keepdims=True))
-
-        def step(k, _):
+                parts = [factor[pl.ds(8 * i, 8), where] * inner[i] for i in range(8)]
+                while len(parts) > 1:
+                    parts = [parts[i] + parts[i + 1] for i in range(0, len(parts), 2)]
+                store(there, h, jnp.sum(parts[0], axis=0, keepdims=True))
+
+        def place_of(k):
             xx = lax.rem(x + pick(k, [o[0] for o in OFFSETS]), 4)
             yy = lax.rem(y + pick(k, [o[1] for o in OFFSETS]), 4)
-            for c in range(2):
-                term_of(c * 16 + xx * 4 + yy)
-                send(c, xx * 4 + yy, k)
+            return xx * 4 + yy
+
+        def step(j, _):
+            ks = [1 + GROUP * j + i for i in range(GROUP)]
+            places = [place_of(k) for k in ks]
+            for place in places:
+                for c in range(2):
+                    term_of(c * 16 + place)
+            for k, place in zip(ks, places):
+                for c in range(2):
+                    send(c, place, k)
             return _
 
-        lax.fori_loop(0, len(OFFSETS) - 1, step, 0)
+        farthest = xs[OFFSETS[0][0]] * 4 + ys[OFFSETS[0][1]]
+        for c in range(2):
+            term_of(c * 16 + farthest)
+            send(c, farthest, 0)
+        lax.fori_loop(0, (len(OFFSETS) - 2) // GROUP, step, 0)
         term_of((1 - core) * 16 + xy)
         send(1 - core, xy, len(OFFSETS) - 1)
         term_of(m)
@@ -276,7 +289,7 @@
         last[there, h] = row
 
     def send_last(c, there, k, places=(*Z_OFFSETS, 0)):
-        distance = pick(k, [hops(o) for o in OFFSETS]) if k is not len(OFFSETS) - 1 else 0
+        distance = hops(OFFSETS[k]) if isinstance(k, int) else pick(k, [hops(o) for o in OFFSETS])
         for i, o in enumerate(places):
             half = lax.div(zs[o], 2)
             pltpu.make_async_remote_copy(
@@ -292,17 +305,12 @@
         return [jnp.sum(v, axis=1, keepdims=True) for v in totals]
 
     loads[2].wait()
-    totals = none
-    for group in ((0, 1, 2), (3,), (4,)):
-        for distance in group:
-            arrived_from(chunk_sem, chunk_in, distance)
-        members = [o for o in OFFSETS if hops(o) in group]
-        totals = add_products(
-            factor, totals, len(members),
-            lambda k: (lax.rem(x + pick(k, [o[0] for o in members]), 4) * 4
-                       + lax.rem(y + pick(k, [o[1] for o in members]), 4)),
-            lambda i, s: chunk_in[(s // 4) * 16 + i, s % 4:s % 4 + 1],
-        )
+    for distance in range(HOPS):
+        arrived_from(chunk_sem, chunk_in, distance)
+    totals = add_products(
+        factor, none, 16, lambda k: k,
+        lambda i, s: chunk_in[(s // 4) * 16 + i, s % 4:s % 4 + 1],
+    )
     transposed(summed_lanes(totals), store_term, send_term)
     term_in[m] = term[m]
 

time: 45.1 us -> 44.7 us (level)
  no operation moved by 1% of the time
where the time goes in v4:
time: 44.7 us
  Pallas kernels  44 us (98%)
  local copies, waits for them, and re-layouts  0.63 us (1%)
    pallas_call x1, Pallas kernels, shards(): pl.pallas_call(kernel, out_shape=jax.ShapeDtypeStruct((RD, CD), f32), in_...  44 us

profile of v4, /device:TPU:1, one launch (start us, length us, event | category | flops | bytes accessed | tf_op | source)
XLA Modules:
  0.0 44.7 jit_solution(12888817227773340832)
XLA Ops:
  0.0 44.0 %shard_map.37 = f32[32,512]{1,0:T(8,128)S(1)} custom-call(f32[32,512]{1,0:T(8,128)} %right_ref.1, f32[32,512]{1,0:T(8,128)} %diag_ref.1, f32[64,16384]{1,0:T(8,128)} %factor_ref.1), custom_call_target="tpu_custom_call" | custom-call | tf_op jit(solution)/shard_map/pallas_call | solution.py:418
  44.0 0.6 %copy.5 = f32[32,512]{1,0:T(8,128)} copy(f32[32,512]{1,0:T(8,128)S(1)} %shard_map.37) | data formatting | bytes 131072

commit v5 on v4

--- a/solution.py
+++ b/solution.py
@@ -127,7 +127,7 @@
     cells, factor, smooth, scale_ref, result,
     row_ref, row_in, chunk_ref, chunk_in, term, term_in, part, part_in,
     fix, fix_in, rhs_ref, last, last_in,
-    load_sem, halo_send, halo_recv, send_sem, recv_sem, chunk_sem, fix_sem, last_sem,
+    load_sem, halo_send, halo_recv, send_sem, recv_sem, last_sem,
 ):
     g, t = lax.axis_index("grp"), lax.axis_index("tile")
     z_hi, core = lax.div(g, 2), lax.rem(g, 2)
@@ -139,10 +139,10 @@
     ys = [lax.rem(y + b, 4) for b in range(4)]
     zs = [lax.rem(z + c, 8) for c in range(8)]
     mates = [
-        (hops(o), (z_hi * 2 + c, xs[o[0]] * 8 + ys[o[1]] * 2 + z_lo))
+        (z_hi * 2 + c, xs[o[0]] * 8 + ys[o[1]] * 2 + z_lo)
         for o in OFFSETS[:-1] for c in range(2)
     ]
-    mates.append((0, (z_hi * 2 + 1 - core, t)))
+    mates.append((z_hi * 2 + 1 - core, t))
     column_mates = [
         (zs[c], (lax.div(zs[c], 2) * 2 + core, xy * 2 + lax.rem(zs[c], 2))) for c in Z_OFFSETS
     ]
@@ -151,7 +151,7 @@
     ]
 
     barrier = pltpu.get_barrier_semaphore()
-    for device in [d for _, d in column_mates] + [d for _, d in mates] + beside_here:
+    for device in [d for _, d in column_mates] + mates + beside_here:
         pl.semaphore_signal(barrier, 1, device_id=device, device_id_type=MESH)
 
     loads = [
@@ -170,20 +170,17 @@
                 device_id=device, device_id_type=MESH,
             ).start()
 
-    def to_m(stage, source, target, near):
-        for distance, device in mates:
+    def to_m(stage, source, target):
+        for device in mates:
             pltpu.make_async_remote_copy(
                 src_ref=source, dst_ref=target.at[m],
-                send_sem=send_sem.at[stage], recv_sem=near.at[distance],
+                send_sem=send_sem.at[stage], recv_sem=recv_sem.at[stage],
                 device_id=device, device_id_type=MESH,
             ).start()
 
     def arrived(sem, target, count):
         blocks = target.at[pl.ds(0, count)]
         pltpu.make_async_copy(blocks, blocks, sem).wait()
-
-    def arrived_from(near, target, distance):
-        arrived(near.at[distance], target, sum(d == distance for d, _ in mates))
 
     def departed(stage, target, count):
         blocks = target.at[pl.ds(0, count)]
@@ -219,7 +216,7 @@
     chunk = jnp.concatenate([row_in[2 * i] + row_in[2 * i + 1] for i in range(4)], axis=0)
     chunk_ref[...] = chunk
     chunk_in[m] = chunk
-    to_m(1, chunk_ref, chunk_in, chunk_sem)
+    to_m(1, chunk_ref, chunk_in)
 
     for halo in halos:
         halo.wait_recv()
@@ -305,8 +302,7 @@
         return [jnp.sum(v, axis=1, keepdims=True) for v in totals]
 
     loads[2].wait()
-    for distance in range(HOPS):
-        arrived_from(chunk_sem, chunk_in, distance)
+    arrived(recv_sem.at[1], chunk_in, N_LANE - 1)
     totals = add_products(
         factor, none, 16, lambda k: k,
         lambda i, s: chunk_in[(s // 4) * 16 + i, s % 4:s % 4 + 1],
@@ -333,10 +329,9 @@
         jnp.concatenate([own, coarse], axis=0),
     )
     fix_in[m] = fix[...]
-    to_m(5, fix, fix_in, fix_sem)
-
-    for distance in range(HOPS):
-        arrived_from(fix_sem, fix_in, distance)
+    to_m(5, fix, fix_in)
+
+    arrived(recv_sem.at[5], fix_in, N_LANE - 1)
     low_rows = lax.broadcasted_iota(jnp.int32, (8, 128), 0) < 4
     field = [jnp.where(low_rows, fix_in[i], fix_in[16 + i]) for i in range(16)]
     around = coarse_neighbours(field)
@@ -389,6 +384,14 @@
         smoothed = 0.2 * smoothed + scale * (residual + beside(smoothed))
     result[...] = (iterate + smoothed)[HR:HR + RD, HC:HC + CD]
 
+    for halo in halos:
+        halo.wait_send()
+    departed(0, row_in, N_Z - 1)
+    departed(1, chunk_in, N_LANE - 1)
+    departed(2, term_in, N_LANE - 1)
+    departed(3, part_in, N_Z - 1)
+    departed(5, fix_in, N_LANE - 1)
+
     row = jnp.zeros((1, 128), jnp.float32)
     for distance in range(HOPS):
         places = [k for k, o in enumerate(OFFSETS) if hops(o) == distance]
@@ -403,13 +406,6 @@
     out_ref[:FAC] = result[:FAC] + pair[0:1]
     out_ref[FAC:] = result[FAC:] + pair[1:2]
 
-    for halo in halos:
-        halo.wait_send()
-    departed(0, row_in, N_Z - 1)
-    departed(1, chunk_in, N_LANE - 1)
-    departed(2, term_in, N_LANE - 1)
-    departed(3, part_in, N_Z - 1)
-    departed(5, fix_in, N_LANE - 1)
     departed(4, last_in, N_GRP * N_TILE - 1)
 
 
@@ -443,9 +439,7 @@
             pltpu.SemaphoreType.DMA((len(DIRECTIONS),)),
             pltpu.SemaphoreType.DMA((len(DIRECTIONS),)),
             pltpu.SemaphoreType.DMA((6,)),
-            pltpu.SemaphoreType.DMA((4,)),
-            pltpu.SemaphoreType.DMA((HOPS,)),
-            pltpu.SemaphoreType.DMA((HOPS,)),
+            pltpu.SemaphoreType.DMA((6,)),
             pltpu.SemaphoreType.DMA((HOPS,)),
         ],
         compiler_params=pltpu.CompilerParams(

time: 44.7 us -> 44.6 us (level)
  no operation moved by 1% of the time
where the time goes in v5:
time: 44.6 us
  Pallas kernels  43.9 us (98%)
  local copies, waits for them, and re-layouts  0.63 us (1%)
    pallas_call x1, Pallas kernels, shards(): pl.pallas_call(kernel, out_shape=jax.ShapeDtypeStruct((RD, CD), f32), in_...  43.9 us

profile of v5, /device:TPU:1, one launch (start us, length us, event | category | flops | bytes accessed | tf_op | source)
XLA Modules:
  0.0 44.6 jit_solution(5302876974641081440)
XLA Ops:
  0.0 43.9 %shard_map.37 = f32[32,512]{1,0:T(8,128)S(1)} custom-call(f32[32,512]{1,0:T(8,128)} %right_ref.1, f32[32,512]{1,0:T(8,128)} %diag_ref.1, f32[64,16384]{1,0:T(8,128)} %factor_ref.1), custom_call_target="tpu_custom_call" | custom-call | tf_op jit(solution)/shard_map/pallas_call | solution.py:414
  43.9 0.6 %copy.5 = f32[32,512]{1,0:T(8,128)} copy(f32[32,512]{1,0:T(8,128)S(1)} %shard_map.37) | data formatting | bytes 131072

commit v6 on v5

--- a/solution.py
+++ b/solution.py
@@ -126,7 +126,7 @@
     right_ref, diag_ref, factor_ref, out_ref,
     cells, factor, smooth, scale_ref, result,
     row_ref, row_in, chunk_ref, chunk_in, term, term_in, part, part_in,
-    fix, fix_in, rhs_ref, last, last_in,
+    side, side_in, side_chunk, side_all, fix, fix_in, rhs_ref, weight_ref, last, last_in,
     load_sem, halo_send, halo_recv, send_sem, recv_sem, last_sem,
 ):
     g, t = lax.axis_index("grp"), lax.axis_index("tile")
@@ -232,9 +232,10 @@
         smoothed = 0.2 * smoothed + scale * (right_side + beside(smoothed))
     smooth[...] = smoothed
     left_over = right_side - (6.0 + diagonal) * smoothed + beside(smoothed)
-    part[4:5] = restricted(left_over[HR:HR + RD, HC:HC + CD], z_lo)
-    part[5:6] = restricted(diagonal[HR:HR + RD, HC:HC + CD], z_lo)
-    part[6:8] = jnp.zeros((2, 128), jnp.float32)
+    side[0:1] = restricted(left_over[HR:HR + RD, HC:HC + CD], z_lo)
+    side[1:2] = restricted(diagonal[HR:HR + RD, HC:HC + CD], z_lo)
+    side_in[z] = side[...]
+    to_z(6, lambda there: side, side_in)
 
     def transposed(inner, store, send):
         inner = [jnp.broadcast_to(v, (8, 128)) for v in inner]
@@ -310,34 +311,43 @@
     transposed(summed_lanes(totals), store_term, send_term)
     term_in[m] = term[m]
 
+    arrived(recv_sem.at[6], side_in, N_Z - 1)
+    rest, mean_diag = (
+        jnp.concatenate(
+            [side_in[2 * i][r:r + 1] + side_in[2 * i + 1][r:r + 1] for i in range(4)], axis=0
+        )
+        for r in range(2)
+    )
+    side_chunk[...] = jnp.where(
+        core == 0,
+        jnp.concatenate([rest, mean_diag], axis=0),
+        jnp.concatenate([mean_diag, rest], axis=0),
+    )
+    side_all[m] = side_chunk[...]
+    to_m(7, side_chunk, side_all)
+
     arrived(recv_sem.at[2], term_in, N_LANE - 1)
-    part[0:4] = jnp.sum(term_in[...], axis=0)
+    part[...] = jnp.sum(term_in[...], axis=0)
     part_in[z] = part[...]
     to_z(3, lambda there: part, part_in)
 
+    low_rows = lax.broadcasted_iota(jnp.int32, (8, 128), 0) < 4
+    arrived(recv_sem.at[7], side_all, N_LANE - 1)
+    for i in range(16):
+        low, high = side_all[i], side_all[16 + i]
+        rhs_ref[i] = jnp.where(low_rows, low, high)
+        weight_ref[i] = 0.5 * (126.0 / 256.0 + pltpu.roll(jnp.where(low_rows, high, low), 4, 0))
+
     arrived(recv_sem.at[3], part_in, N_Z - 1)
-    parts = [part_in[i] for i in range(N_Z)]
-    coarse = functools.reduce(jnp.add, [v[0:4] for v in parts])
-    rest = jnp.concatenate([parts[2 * i][4:5] + parts[2 * i + 1][4:5] for i in range(4)], axis=0)
-    mean_diag = jnp.concatenate(
-        [parts[2 * i][5:6] + parts[2 * i + 1][5:6] for i in range(4)], axis=0
-    )
-    own = rest - 0.5 * (126.0 / 256.0 + mean_diag) * coarse
-    fix[...] = jnp.where(
-        core == 0,
-        jnp.concatenate([coarse, own], axis=0),
-        jnp.concatenate([own, coarse], axis=0),
-    )
+    fix[...] = functools.reduce(jnp.add, [part_in[i] for i in range(N_Z)])
     fix_in[m] = fix[...]
     to_m(5, fix, fix_in)
 
     arrived(recv_sem.at[5], fix_in, N_LANE - 1)
-    low_rows = lax.broadcasted_iota(jnp.int32, (8, 128), 0) < 4
-    field = [jnp.where(low_rows, fix_in[i], fix_in[16 + i]) for i in range(16)]
+    field = [jnp.concatenate([fix_in[i], fix_in[16 + i]], axis=0) for i in range(16)]
     around = coarse_neighbours(field)
     for i in range(16):
-        own_i = pltpu.roll(jnp.where(low_rows, fix_in[16 + i], fix_in[i]), 4, 0)
-        rhs_ref[i] = own_i + (0.5 / 256.0) * around[i]
+        rhs_ref[i] = rhs_ref[i] - weight_ref[i] * field[i] + (0.5 / 256.0) * around[i]
     totals = add_products(factor, none, 16, lambda k: k, lambda i, s: rhs_ref[i, s:s + 1])
     transposed(summed_lanes(totals), store_last, send_last)
     send_last(core, xy, len(OFFSETS) - 1, Z_OFFSETS)
@@ -352,7 +362,7 @@
             gg = g + a
             ok = ok_t & (gg >= 0) & (gg < N_GRP)
             gg = (gg + N_GRP) % N_GRP
-            row = fix_in[(gg % 2) * 16 + tt // 2, pl.ds((gg % 2) * 4 + gg // 2, 1)]
+            row = fix_in[(gg % 2) * 16 + tt // 2, pl.ds(gg // 2, 1)]
             rows.append(quarter(row, tt % 2, i_hi, ok))
         return jnp.concatenate(rows + [jnp.zeros((4, 128), jnp.float32)], axis=0)
 
@@ -390,6 +400,8 @@
     departed(1, chunk_in, N_LANE - 1)
     departed(2, term_in, N_LANE - 1)
     departed(3, part_in, N_Z - 1)
+    departed(6, side_in, N_Z - 1)
+    departed(7, side_all, N_LANE - 1)
     departed(5, fix_in, N_LANE - 1)
 
     row = jnp.zeros((1, 128), jnp.float32)
@@ -428,18 +440,23 @@
             pltpu.VMEM((N_LANE, 4, 128), f32),
             pltpu.VMEM((N_LANE, 4, 128), f32),
             pltpu.VMEM((N_LANE, 4, 128), f32),
-            pltpu.VMEM((8, 128), f32),
-            pltpu.VMEM((N_Z, 8, 128), f32),
+            pltpu.VMEM((4, 128), f32),
+            pltpu.VMEM((N_Z, 4, 128), f32),
+            pltpu.VMEM((2, 128), f32),
+            pltpu.VMEM((N_Z, 2, 128), f32),
             pltpu.VMEM((8, 128), f32),
             pltpu.VMEM((N_LANE, 8, 128), f32),
+            pltpu.VMEM((4, 128), f32),
+            pltpu.VMEM((N_LANE, 4, 128), f32),
+            pltpu.VMEM((16, 8, 128), f32),
             pltpu.VMEM((16, 8, 128), f32),
             pltpu.VMEM((N_LANE, 4, 1, 128), f32),
             pltpu.VMEM((N_GRP * N_TILE, 1, 128), f32),
             pltpu.SemaphoreType.DMA((3,)),
             pltpu.SemaphoreType.DMA((len(DIRECTIONS),)),
             pltpu.SemaphoreType.DMA((len(DIRECTIONS),)),
-            pltpu.SemaphoreType.DMA((6,)),
-            pltpu.SemaphoreType.DMA((6,)),
+            pltpu.SemaphoreType.DMA((8,)),
+            pltpu.SemaphoreType.DMA((8,)),
             pltpu.SemaphoreType.DMA((HOPS,)),
         ],
         compiler_params=pltpu.CompilerParams(

time: 44.6 us -> 44.4 us (level)
  no operation moved by 1% of the time
where the time goes in v6:
time: 44.4 us; the launch traced here: 44.3 us
  Pallas kernels  43.7 us (98%)
  local copies, waits for them, and re-layouts  0.63 us (1%)
    pallas_call x1, Pallas kernels, shards(): pl.pallas_call(kernel, out_shape=jax.ShapeDtypeStruct((RD, CD), f32), in_...  43.7 us

profile of v6, /device:TPU:1, one launch (start us, length us, event | category | flops | bytes accessed | tf_op | source)
XLA Modules:
  0.0 44.3 jit_solution(13015494351849121528)
XLA Ops:
  0.0 43.7 %shard_map.37 = f32[32,512]{1,0:T(8,128)S(1)} custom-call(f32[32,512]{1,0:T(8,128)} %right_ref.1, f32[32,512]{1,0:T(8,128)} %diag_ref.1, f32[64,16384]{1,0:T(8,128)} %factor_ref.1), custom_call_target="tpu_custom_call" | custom-call | tf_op jit(solution)/shard_map/pallas_call | solution.py:426
  43.7 0.6 %copy.5 = f32[32,512]{1,0:T(8,128)} copy(f32[32,512]{1,0:T(8,128)S(1)} %shard_map.37) | data formatting | bytes 131072
